TPU v7x, 32 devices: a whole 2x2x4 slice. The times are simulated.
32 devices in a mesh: clip: 2 (over x), frame: 16 (over z, y, core).
Axes of the slice: x: 2, y: 2, z: 4, core: 2. Of those that a mesh axis runs over, the one named last changes fastest.
Arguments:
- cotangent: bfloat16 [32, 64, 512], P(('clip', 'frame')), parts along dimension 0, may hold values from -6 to 6
- q_spatial: bfloat16 [32, 64, 512], P(('clip', 'frame')), parts along dimension 0, may hold values from -48 to 48
- k_spatial: bfloat16 [32, 64, 512], P(('clip', 'frame')), parts along dimension 0, may hold values from -48 to 48
- v_spatial: bfloat16 [32, 64, 512], P(('clip', 'frame')), parts along dimension 0, may hold values from -6 to 6
- q_temporal: bfloat16 [32, 64, 512], P('clip', 'frame'), parts along dimension 0, may hold values from -48 to 48
- k_temporal: bfloat16 [32, 64, 512], P('clip', 'frame'), parts along dimension 0, may hold values from -48 to 48
- v_temporal: bfloat16 [32, 64, 512], P('clip', 'frame'), parts along dimension 0, may hold values from -6 to 6
- w_qkv_spatial: bfloat16 [512, 1536], replicated, may hold values from -0.25 to 0.25
- w_out_spatial: bfloat16 [512, 512], replicated, may hold values from -0.25 to 0.25
- w_qkv_temporal: bfloat16 [512, 1536], replicated, may hold values from -0.25 to 0.25
- w_out_temporal: bfloat16 [512, 512], replicated, may hold values from -0.25 to 0.25
Outputs:
- input_grad: bfloat16 [32, 64, 512], P(('clip', 'frame')), parts along dimension 0
- grad_out_spatial: float32 [1024, 512], P('clip'), parts along dimension 0
- grad_out_temporal: float32 [1024, 512], P('clip'), parts along dimension 0
There are 2 independent parts, one for each index of `clip`. A program takes and returns all parts, laid end to end along the dimension named above; an argument that names none is the same for every part. Nothing has to cross between parts.
All inputs are finite; a program needn't handle non-finite values.
Results may differ from a plain program's by a relative error of at most 0.0079.
Values may be sent and summed in bfloat16 or wider, within the bound.
A program may use at most 64 MiB of HBM per device.

v0:
```python
import math

import jax
import jax.numpy as jnp
from jax import lax
from jax.sharding import PartitionSpec as P

D = 512
HEADS = 8


def contract_last(left_side, right_side):
    return lax.dot_general(
        left_side, right_side, (((1,), (1,)), ((), ())), preferred_element_type=jnp.float32
    )


def contract_first(left_side, right_side):
    return lax.dot_general(
        left_side, right_side, (((0,), (0,)), ((), ())), preferred_element_type=jnp.float32
    )


def heads_view(array):
    return array.reshape(array.shape[:-1] + (HEADS, D // HEADS))


def attention_back(query_rows, key_rows, value_rows, upstream, score_scale, temporal):
    side_q = "qbhd" if temporal else "bqhd"
    side_k = "kbhd" if temporal else "bkhd"
    scores = (
        jnp.einsum(
            side_q + "," + side_k + "->bhqk",
            query_rows,
            key_rows,
            preferred_element_type=jnp.float32,
        )
        * score_scale
    )
    probs = jax.nn.softmax(scores, axis=-1)
    probs_half = probs.astype(jnp.bfloat16)
    mixed = jnp.einsum(
        "bhqk," + side_k + "->" + side_q, probs_half, value_rows, preferred_element_type=jnp.float32
    ).astype(jnp.bfloat16)
    d_probs = jnp.einsum(
        side_q + "," + side_k + "->bhqk", upstream, value_rows, preferred_element_type=jnp.float32
    )
    d_scores = (
        probs * (d_probs - jnp.sum(probs * d_probs, axis=-1, keepdims=True)) * score_scale
    ).astype(jnp.bfloat16)
    grad_query = jnp.einsum(
        "bhqk," + side_k + "->" + side_q, d_scores, key_rows, preferred_element_type=jnp.float32
    ).astype(jnp.bfloat16)
    grad_key = jnp.einsum(
        "bhqk," + side_q + "->" + side_k, d_scores, query_rows, preferred_element_type=jnp.float32
    ).astype(jnp.bfloat16)
    grad_value = jnp.einsum(
        "bhqk," + side_q + "->" + side_k, probs_half, upstream, preferred_element_type=jnp.float32
    ).astype(jnp.bfloat16)
    return (mixed, grad_query, grad_key, grad_value)


def project_back(base_rows, cotangent_parts, weights):
    summed = base_rows.astype(jnp.float32)
    for position in range(3):
        summed = summed + contract_last(
            cotangent_parts[position].reshape(-1, D), weights[:, position * D : (position + 1) * D]
        )
    return summed


def on_device(
    cotangent,
    q_spatial,
    k_spatial,
    v_spatial,
    q_temporal,
    k_temporal,
    v_temporal,
    w_qkv_spatial,
    w_out_spatial,
    w_qkv_temporal,
    w_out_temporal,
):
    frames_here, patches, model_width = cotangent.shape
    score_scale = 1.0 / math.sqrt(D // HEADS)
    flat_rows = cotangent.reshape(-1, model_width)
    d_mixed = (
        contract_last(flat_rows, w_out_spatial)
        .astype(jnp.bfloat16)
        .reshape(frames_here, patches, model_width)
    )
    mixed_s, grad_q, grad_k, grad_v = attention_back(
        heads_view(q_spatial),
        heads_view(k_spatial),
        heads_view(v_spatial),
        heads_view(d_mixed),
        score_scale,
        False,
    )
    grad_spatial = contract_first(mixed_s.reshape(-1, model_width), flat_rows)
    inner_grad = project_back(flat_rows, (grad_q, grad_k, grad_v), w_qkv_spatial).astype(
        jnp.bfloat16
    )
    inner_frames = inner_grad.reshape(frames_here, patches, model_width)
    patch_rows = lax.all_to_all(inner_frames, "frame", split_axis=1, concat_axis=0, tiled=True)
    frames, pieces, _ = patch_rows.shape
    patch_flat = patch_rows.reshape(-1, model_width)
    d_mixed_t = (
        contract_last(patch_flat, w_out_temporal)
        .astype(jnp.bfloat16)
        .reshape(frames, pieces, model_width)
    )
    mixed_t, grad_tq, grad_tk, grad_tv = attention_back(
        heads_view(q_temporal),
        heads_view(k_temporal),
        heads_view(v_temporal),
        heads_view(d_mixed_t),
        score_scale,
        True,
    )
    grad_temporal = contract_first(mixed_t.reshape(-1, model_width), patch_flat)
    patch_result = (
        project_back(patch_flat, (grad_tq, grad_tk, grad_tv), w_qkv_temporal)
        .astype(jnp.bfloat16)
        .reshape(frames, pieces, model_width)
    )
    result = lax.all_to_all(patch_result, "frame", split_axis=0, concat_axis=1, tiled=True)
    weight_grads = lax.psum((grad_spatial, grad_temporal), "frame")
    grad_norm = math.sqrt(frames * patches)
    return (result, weight_grads[0] / grad_norm, weight_grads[1] / grad_norm)


def solution(mesh):
    return jax.shard_map(
        on_device,
        mesh=mesh,
        in_specs=(
            P(("clip", "frame"), None, None),
            P(("clip", "frame"), None, None),
            P(("clip", "frame"), None, None),
            P(("clip", "frame"), None, None),
            P("clip", "frame", None),
            P("clip", "frame", None),
            P("clip", "frame", None),
            P(),
            P(),
            P(),
            P(),
        ),
        out_specs=(P(("clip", "frame"), None, None), P("clip", None), P("clip", None)),
        check_vma=False,
    )
```

profile of v0, /device:TPU:0, one launch (start us, length us, event | category | flops | bytes accessed | tf_op | source)
XLA Modules:
  0.0 141.3 jit_solution(5572912268341521570)
XLA Ops:
  7.2 1.0 copy-done
  8.2 1.1 convolution_convert_fusion.9
  9.5 1.0 reshape.132
  10.4 1.0 reshape.133
  11.4 1.0 reshape.135
  12.4 0.2 fusion.54
  12.6 0.2 fusion.116
  12.8 0.2 convolution_convert_fusion.5
  13.1 0.2 fusion.17
  13.3 0.3 fusion.16
  13.7 0.1 reshape.136
  13.9 0.1 reshape.137
  14.0 0.4 copy-done.2
  14.4 0.3 convolution_add_fusion.5
  14.7 0.3 convolution_add_fusion.4
  15.0 0.3 fusion.25
  15.4 0.5 broadcast.68
  16.0 1.0 reduce.6
  17.0 0.7 reshape.150
  17.6 7.4 %all-to-all-start = ((bf16[16,2,1024]{2,1,0:T(2,128)(2,1)}), bf16[16,2,1024]{2,1,0:T(2,128)(2,1)S(1)}, u32[]{:S(2)}, u32[]{:S(2)}) async-start(bf16[16,2,1024]{2,1,0:T(2,128)(2,1)} %reshape.150), calls=%async_computation | async-start | bytes 131072 | tf_op jit(solution)/shard_map/all_to_all | solution.py:106
  25.1 0.2 fusion.20
  25.3 0.1 reshape.141
  25.5 0.1 reshape.142
  25.6 0.1 reshape.143
  25.8 0.1 reshape.148
  26.0 1.3 fusion.63
  27.3 0.3 fusion.121
  27.6 0.4 fusion.21
  28.0 0.1 reshape.149
  28.2 3.8 %all-to-all-done = bf16[16,2,1024]{2,1,0:T(2,128)(2,1)S(1)} async-done(((bf16[16,2,1024]{2,1,0:T(2,128)(2,1)}), bf16[16,2,1024]{2,1,0:T(2,128)(2,1)S(1)}, u32[]{:S(2)}, u32[]{:S(2)}) %all-to-all-start) | async-done | bytes 65568 | tf_op jit(solution)/shard_map/all_to_all | solution.py:106
  32.0 0.3 convolution_convert_fusion.8
  32.3 0.1 reshape_reshape.4
  32.4 0.2 fusion.45
  32.6 0.4 fusion.22
  33.1 0.1 reshape.146
  33.2 0.3 fusion.18
  33.6 0.1 reshape.144
  33.7 1.3 fusion.60
  35.0 0.2 fusion.19
  35.3 0.1 reshape.145
  35.5 1.0 copy-done.1
  36.4 0.3 convolution_add_fusion.2
  36.7 0.3 convolution_add_fusion.1
  37.0 0.3 fusion.24
  37.3 10.7 %all_to_all.21 = bf16[16,4,512]{2,1,0:T(4,128)(2,1)S(1)} all-to-all(bf16[16,4,512]{2,1,0:T(4,128)(2,1)S(1)} %reshape.147), channel_id=1, replica_groups=mesh['clip'=2,'frame'=16] {'frame'}, dimensions={0} | all-to-all | bytes 131072 | tf_op jit(solution)/shard_map/all_to_all | solution.py:128
  48.0 0.6 all_to_all.8
  48.7 82.7 %all-reduce.3.cloned.1.call-done = (f32[512,512]{1,0:T(8,128)}, f32[512,512]{1,0:T(8,128)}) async-done(((f32[512,512]{1,0:T(8,128)}, f32[512,512]{1,0:T(8,128)}), (f32[512,512]{1,0:T(8,128)}, f32[512,512]{1,0:T(8,128)})) %all-reduce.3.cloned.1.call-update) | async-done | bytes 2097168 | tf_op jit(solution)/shard_map/psum | solution.py:129
  131.4 3.1 %broadcast_multiply_fusion = (f32[512,512]{1,0:T(8,128)}, f32[512,512]{1,0:T(8,128)}) fusion(f32[512,512]{1,0:T(8,128)} %get-tuple-element.4, f32[512,512]{1,0:T(8,128)} %get-tuple-element.3), kind=kLoop, calls=%fused_computation.44 | loop fusion | flops 524288 | bytes 4194304 | tf_op jit(solution)/shard_map/div | solution.py:131
  (26 shorter events, 0.8 us)
Async XLA Ops:
  7.2 1.0 copy-start
  13.0 1.4 copy-start.2
  13.0 1.4 copy-start.3
  14.7 10.6 %copy-start.5 = (bf16[16,4,512]{2,1,0:T(4,128)(2,1)S(1)}, bf16[16,4,512]{2,1,0:T(4,128)(2,1)}, u32[]{:S(2)}) copy-start(bf16[16,4,512]{2,1,0:T(4,128)(2,1)} %param.15) | copy-start | bytes 196612
  15.0 10.4 %copy-start.6 = (bf16[16,4,512]{2,1,0:T(4,128)(2,1)S(1)}, bf16[16,4,512]{2,1,0:T(4,128)(2,1)}, u32[]{:S(2)}) copy-start(bf16[16,4,512]{2,1,0:T(4,128)(2,1)} %param.16) | copy-start | bytes 196612
  15.0 10.6 %copy-start.7 = (bf16[16,4,512]{2,1,0:T(4,128)(2,1)S(1)}, bf16[16,4,512]{2,1,0:T(4,128)(2,1)}, u32[]{:S(2)}) copy-start(bf16[16,4,512]{2,1,0:T(4,128)(2,1)} %param.17) | copy-start | bytes 196612
  17.6 14.3 %all-to-all-start = ((bf16[16,2,1024]{2,1,0:T(2,128)(2,1)}), bf16[16,2,1024]{2,1,0:T(2,128)(2,1)S(1)}, u32[]{:S(2)}, u32[]{:S(2)}) async-start(bf16[16,2,1024]{2,1,0:T(2,128)(2,1)} %reshape.150), calls=%async_computation | async-start | bytes 131072 | tf_op jit(solution)/shard_map/all_to_all | solution.py:106
  25.0 106.3 %all-reduce.3.cloned.1.call-start = ((), (), s32[]{:S(2)}) async-start(), calls=%async_computation.2 | async-start | bytes 4194304 | tf_op jit(solution)/shard_map/psum | solution.py:129
  27.3 4.7 %copy-start.4 = (bf16[512,512]{1,0:T(8,128)(2,1)S(1)}, bf16[512,512]{1,0:T(8,128)(2,1)}, u32[]{:S(2)}) copy-start(bf16[512,512]{1,0:T(8,128)(2,1)} %param.21) | copy-start | bytes 1572868
  35.0 1.4 copy-start.1
Sparse Core Ops, SparseCore 0:
  35.1 96.2 all-reduce.2
where the time goes:
time: 142 us; the launch traced here: 141 us
  waiting for transfers between devices  86.5 us (61%)
  between operations  14.3 us (10%)
  blocking collectives  10.7 us (8%)
  local copies, waits for them, and re-layouts  9.42 us (7%)
  matrix products  8.82 us (6%)
  starting transfers between devices  7.43 us (5%)
  other arithmetic  4.09 us (3%)
    psum x1, waiting for transfers between devices, on_device(): weight_grads = lax.psum((grad_spatial, grad_temporal), 'frame')  82.7 us
    all_to_all x1, blocking collectives, on_device(): lax.all_to_all(patch_result, 'frame', split_axis=0, concat_axis=1, tiled=...  10.7 us
    all_to_all x1, starting transfers between devices, on_device(): lax.all_to_all(inner_frames, 'frame', split_axis=1, concat_axis=0, tiled=...  7.39 us
    all_to_all x1, waiting for transfers between devices, on_device(): lax.all_to_all(inner_frames, 'frame', split_axis=1, concat_axis=0, tiled=...  3.76 us
    unnamed x19, local copies, waits for them, and re-layouts  3.67 us
    dot_general x8, matrix products, contract_last(): lax.dot_general(left_side, right_side, (((1,), (1,)), ((), ())), preferre...  3.1 us
    div x1, other arithmetic, on_device(): return (result, weight_grads[0] / grad_norm, weight_grads[1] / grad_norm)  3.09 us
  transfers between devices with their start and end apart: 2, of which 2 were waited for; matrix products, arithmetic and copies ran while one was open for 3% of the time, Pallas kernels for 0%

commit v1 on v0

v1 whole, which is shorter than its diff:
```python
import functools
import math

import jax
import jax.numpy as jnp
from jax import lax
from jax.experimental import pallas as pl
from jax.experimental.pallas import tpu as pltpu
from jax.sharding import PartitionSpec as P

D = 512
HEADS = 8
HEAD_DIM = D // HEADS
LANES = 128
BF16 = jnp.bfloat16
F32 = jnp.float32


def dot_nt(a, b):
    return lax.dot_general(a, b, (((1,), (1,)), ((), ())), preferred_element_type=F32)


def dot_tn(a, b):
    return lax.dot_general(a, b, (((0,), (0,)), ((), ())), preferred_element_type=F32)


def dot_nn(a, b):
    return lax.dot_general(a, b, (((1,), (0,)), ((), ())), preferred_element_type=F32)


def reduce_levels(n):
    levels, stride = [], 1
    for _ in range(2):
        if n // stride > 2 and (n // stride) % 2 == 0:
            levels.append((stride, 2))
            stride *= 2
    levels.append((stride, n // stride))
    return levels


def padded_rows(n):
    return n * 16 * pl.cdiv(D, n * 16)


def head_stack(tile, group_masks):
    return jnp.concatenate([tile * mask for mask in group_masks], axis=0)


def head_select(stacked, tokens, lane):
    out = stacked[:tokens]
    for g in range(1, LANES // HEAD_DIM):
        out = jnp.where(lane >= g * HEAD_DIM, stacked[g * tokens : (g + 1) * tokens], out)
    return out


def attention_forward(q, k, v, scale, group_masks, lane, same):
    tokens = q.shape[0]
    probs, mixed = [], []
    for t in range(D // LANES):
        cols = slice(t * LANES, (t + 1) * LANES)
        scores = dot_nt(k[:, cols], head_stack(q[:, cols], group_masks)) * scale
        if same is not None:
            scores = jnp.where(same, scores, -1e30)
        e = jnp.exp(scores - jnp.max(scores, axis=0, keepdims=True))
        p = e / jnp.sum(e, axis=0, keepdims=True)
        probs.append(p)
        mixed.append(head_select(dot_tn(p.astype(BF16), v[:, cols]), tokens, lane).astype(BF16))
    return probs, jnp.concatenate(mixed, axis=1)


def attention_backward(q, k, v, d_mixed, probs, scale, group_masks, lane):
    tokens = q.shape[0]
    dq, dk, dv = [], [], []
    for t in range(D // LANES):
        cols = slice(t * LANES, (t + 1) * LANES)
        p = probs[t]
        up = head_stack(d_mixed[:, cols], group_masks)
        d_probs = dot_nt(v[:, cols], up)
        row = jnp.sum(p * d_probs, axis=0, keepdims=True)
        d_scores = (p * (d_probs - row) * scale).astype(BF16)
        dq.append(head_select(dot_tn(d_scores, k[:, cols]), tokens, lane).astype(BF16))
        dk.append(dot_nn(d_scores, head_stack(q[:, cols], group_masks)).astype(BF16))
        dv.append(dot_nn(p.astype(BF16), up).astype(BF16))
    return jnp.concatenate(dq + dk + dv, axis=1)


class GradSum:
    def __init__(self, n, me, acc, send, out, recv, sems, divisor):
        self.levels = reduce_levels(n)
        self.me, self.acc, self.send, self.out = me, acc, send, out
        self.recv, self.sems, self.divisor = recv, sems, divisor
        self.rows, self.offsets = [padded_rows(n)], [0]
        for stride, size in self.levels:
            part = self.rows[-1] // size
            self.rows.append(part)
            self.offsets.append(self.offsets[-1] + lax.rem(lax.div(me, stride), size) * part)
        self.pending = None

    def span(self, offset, rows):
        return pl.ds(pl.multiple_of(offset, rows), rows)

    def peers(self, level):
        stride, size = self.levels[level]
        mine = lax.rem(lax.div(self.me, stride), size)
        for d in range(1, size):
            other = lax.rem(mine + d, size)
            yield d, other, self.me + (other - mine) * stride

    def start_reduce(self, level):
        rows = self.rows[level + 1]
        copies = []
        for d, other, device in self.peers(level):
            copy = pltpu.make_async_remote_copy(
                src_ref=self.send.at[self.span(self.offsets[level] + other * rows, rows)],
                dst_ref=self.recv[level].at[d - 1],
                send_sem=self.sems[0].at[level, d - 1],
                recv_sem=self.sems[1].at[level, d - 1],
                device_id={"frame": device},
                device_id_type=pl.DeviceIdType.MESH,
            )
            copy.start()
            copies.append(copy)
        self.pending = copies

    def begin(self, partial):
        self.acc[:D, :] = partial
        self.send[:D, :] = partial.astype(BF16)
        if self.rows[0] > D:
            self.acc[D:, :] = jnp.zeros((self.rows[0] - D, D), F32)
            self.send[D:, :] = jnp.zeros((self.rows[0] - D, D), BF16)
        self.start_reduce(0)

    def finish_reduce(self, level):
        for copy in self.pending:
            copy.wait()
        rows = self.rows[level + 1]
        span = self.span(self.offsets[level + 1], rows)
        total = self.acc[span, :]
        for d, _, _ in self.peers(level):
            total = total + self.recv[level][d - 1].astype(F32)
        if level + 1 < len(self.levels):
            self.acc[span, :] = total
            self.send[span, :] = total.astype(BF16)
            self.start_reduce(level + 1)
        else:
            self.out[span, :] = (total / self.divisor).astype(BF16)
            self.start_gather(level)

    def start_gather(self, level):
        span = self.span(self.offsets[level + 1], self.rows[level + 1])
        copies = []
        for d, _, device in self.peers(level):
            copy = pltpu.make_async_remote_copy(
                src_ref=self.out.at[span],
                dst_ref=self.out.at[span],
                send_sem=self.sems[2].at[level, d - 1],
                recv_sem=self.sems[3].at[level, d - 1],
                device_id={"frame": device},
                device_id_type=pl.DeviceIdType.MESH,
            )
            copy.start()
            copies.append(copy)
        self.pending = copies

    def finish_gather(self, level):
        for copy in self.pending:
            copy.wait()
        if level > 0:
            self.start_gather(level - 1)


def exchange(n, me, source, target, send_sem, recv_sem):
    copies = []
    for d in range(1, n):
        other = lax.rem(me + d, n)
        copy = pltpu.make_async_remote_copy(
            src_ref=source.at[other],
            dst_ref=target.at[me],
            send_sem=send_sem.at[d - 1],
            recv_sem=recv_sem.at[d - 1],
            device_id={"frame": other},
            device_id_type=pl.DeviceIdType.MESH,
        )
        copy.start()
        copies.append(copy)
    target[me] = source[me]
    return copies


def kernel(n, n_levels, scale, norm, *refs):
    inputs, refs = refs[:11], refs[11:]
    result_ref, grad_s_ref, grad_t_ref = refs[:3]
    refs = refs[3:]
    held, refs = refs[:11], refs[11:]
    load_sem, out_a, in_a, out_b, in_b, a_send, a_recv, b_send, b_recv = refs[:9]
    refs = refs[9:]
    acc_s, send_s = refs[:2]
    recv_s, refs = refs[2 : 2 + n_levels], refs[2 + n_levels :]
    sems_s, refs = refs[:4], refs[4:]
    acc_t, send_t = refs[:2]
    recv_t, refs = refs[2 : 2 + n_levels], refs[2 + n_levels :]
    sems_t = refs[:4]

    me = lax.axis_index("frame")
    loads = []
    for i in (1, 2, 3, 0, 8, 4, 5, 6, 7, 10, 9):
        copy = pltpu.make_async_copy(inputs[i], held[i], load_sem.at[i])
        copy.start()
        loads.append((i, copy))
    loads = dict(loads)

    barrier = pltpu.get_barrier_semaphore()
    for d in range(1, n):
        pl.semaphore_signal(
            barrier,
            inc=1,
            device_id={"frame": lax.rem(me + d, n)},
            device_id_type=pl.DeviceIdType.MESH,
        )

    cot_h, qs_h, ks_h, vs_h, qt_h, kt_h, vt_h, wqs_h, wos_h, wqt_h, wot_h = held
    pieces = qt_h.shape[1]
    lane_row = lax.broadcasted_iota(jnp.int32, (1, LANES), 1)
    masks = [
        jnp.where((lane_row >= g * HEAD_DIM) & (lane_row < (g + 1) * HEAD_DIM), 1.0, 0.0).astype(BF16)
        for g in range(LANES // HEAD_DIM)
    ]

    def flat(ref):
        return jnp.concatenate([ref[j].astype(F32) for j in range(ref.shape[0])], axis=0).astype(BF16)

    for i in (1, 2, 3, 0):
        loads[i].wait()
    cot, q_s, k_s, v_s = cot_h[...], qs_h[...], ks_h[...], vs_h[...]
    tokens = cot.shape[0]
    lane = lax.broadcasted_iota(jnp.int32, (tokens, LANES), 1)
    probs_s, mixed_s = attention_forward(q_s, k_s, v_s, scale, masks, lane, None)
    partial_s = dot_tn(mixed_s, cot)
    pl.semaphore_wait(barrier, n - 1)
    sum_s = GradSum(n, me, acc_s, send_s, grad_s_ref, recv_s, sems_s, norm)
    sum_s.begin(partial_s)

    loads[8].wait()
    d_mixed_s = dot_nt(cot, wos_h[...]).astype(BF16)
    parts_s = attention_backward(q_s, k_s, v_s, d_mixed_s, probs_s, scale, masks, lane)
    loads[7].wait()
    d_x1 = (cot.astype(F32) + dot_nt(parts_s, wqs_h[...])).astype(BF16).astype(F32)
    for j in range(n):
        out_a[j] = d_x1[j * pieces : (j + 1) * pieces].astype(BF16)
    sent_a = exchange(n, me, out_a, in_a, a_send, a_recv)

    sum_s.finish_reduce(0)
    for i in (4, 5, 6):
        loads[i].wait()
    q_t, k_t, v_t = flat(qt_h), flat(kt_h), flat(vt_h)
    rows_t = q_t.shape[0]
    groups = LANES // HEAD_DIM
    key_row = lax.broadcasted_iota(jnp.int32, (rows_t, groups * rows_t), 0)
    query_col = lax.broadcasted_iota(jnp.int32, (rows_t, groups * rows_t), 1)
    same = lax.rem(key_row, pieces) == lax.rem(query_col, pieces)
    lane_t = lax.broadcasted_iota(jnp.int32, (rows_t, LANES), 1)
    probs_t, mixed_t = attention_forward(q_t, k_t, v_t, scale, masks, lane_t, same)
    loads[10].wait()
    loads[9].wait()
    if n_levels > 1:
        sum_s.finish_reduce(1)
    for copy in sent_a:
        copy.wait()
    rows = flat(in_a)

    sum_t = GradSum(n, me, acc_t, send_t, grad_t_ref, recv_t, sems_t, norm)
    sum_t.begin(dot_tn(mixed_t, rows))
    d_mixed_t = dot_nt(rows, wot_h[...]).astype(BF16)
    parts_t = attention_backward(q_t, k_t, v_t, d_mixed_t, probs_t, scale, masks, lane_t)
    d_x0 = rows.astype(F32) + dot_nt(parts_t, wqt_h[...])
    for j in range(n):
        out_b[j] = d_x0[j * pieces : (j + 1) * pieces].astype(BF16)
    sent_b = exchange(n, me, out_b, in_b, b_send, b_recv)

    for level in range(n_levels):
        sum_t.finish_reduce(level)
        if level >= 2:
            sum_s.finish_reduce(level)
    for level in reversed(range(n_levels)):
        sum_s.finish_gather(level)
        sum_t.finish_gather(level)
    for copy in sent_b:
        copy.wait()
    result_ref[...] = flat(in_b)


def on_device(n, *args):
    cotangent, q_temporal = args[0], args[4]
    _, pieces, width = q_temporal.shape
    frames_here, patches, _ = cotangent.shape
    tokens = frames_here * patches
    flat_args = [a.reshape(tokens, width) for a in args[:4]] + list(args[4:])
    levels = reduce_levels(n)
    scratch = [pltpu.VMEM(a.shape, a.dtype) for a in flat_args]
    scratch.append(pltpu.SemaphoreType.DMA((len(flat_args),)))
    scratch += [pltpu.VMEM((n, pieces, width), BF16)] * 4
    scratch += [pltpu.SemaphoreType.DMA((n - 1,))] * 4
    widest = max(size for _, size in levels)
    for _ in range(2):
        scratch += [pltpu.VMEM((padded_rows(n), D), F32), pltpu.VMEM((padded_rows(n), D), BF16)]
        rows = padded_rows(n)
        for _, size in levels:
            rows //= size
            scratch.append(pltpu.VMEM((max(size - 1, 1), rows, D), BF16))
        scratch += [pltpu.SemaphoreType.DMA((len(levels), widest))] * 4
    result, grad_s, grad_t = pl.pallas_call(
        functools.partial(
            kernel,
            n,
            len(levels),
            1.0 / math.sqrt(HEAD_DIM),
            math.sqrt(n * tokens),
        ),
        out_shape=(
            jax.ShapeDtypeStruct((tokens, width), BF16),
            jax.ShapeDtypeStruct((padded_rows(n), D), BF16),
            jax.ShapeDtypeStruct((padded_rows(n), D), BF16),
        ),
        in_specs=[pl.BlockSpec(memory_space=pltpu.HBM)] * len(flat_args),
        out_specs=(pl.BlockSpec(memory_space=pltpu.VMEM),) * 3,
        scratch_shapes=scratch,
        compiler_params=pltpu.CompilerParams(
            collective_id=0, has_side_effects=True, vmem_limit_bytes=40 * 1024 * 1024
        ),
    )(*flat_args)
    return (
        result.reshape(frames_here, patches, width),
        grad_s[:D].astype(F32),
        grad_t[:D].astype(F32),
    )


def solution(mesh):
    n = mesh.shape["frame"]
    return jax.shard_map(
        functools.partial(on_device, n),
        mesh=mesh,
        in_specs=(
            P(("clip", "frame"), None, None),
            P(("clip", "frame"), None, None),
            P(("clip", "frame"), None, None),
            P(("clip", "frame"), None, None),
            P("clip", "frame", None),
            P("clip", "frame", None),
            P("clip", "frame", None),
            P(),
            P(),
            P(),
            P(),
        ),
        out_specs=(P(("clip", "frame"), None, None), P("clip", None), P("clip", None)),
        check_vma=False,
    )
```

time: 142 us -> 54.8 us (0.39)
  waiting for transfers between devices: 86.5 us -> 0 us
  Pallas kernels: 0 us -> 39.9 us
  between operations: 14.3 us -> 0.66 us
  blocking collectives: 10.7 us -> 0 us
  matrix products: 8.82 us -> 0 us
  starting transfers between devices: 7.43 us -> 0 us
  local copies, waits for them, and re-layouts: 9.42 us -> 11.4 us
  other arithmetic: 4.09 us -> 2.21 us
    psum x1 -> x0, waiting for transfers between devices: 82.7 us -> none  [on_device(): weight_grads = lax.psum((grad_spatial, grad_temporal), 'frame')]
    pallas_call x0 -> x1, Pallas kernels: none -> 39.9 us  [on_device(): pl.pallas_call(functools.partial(kernel, n, len(levels), 1.0 / math.sqrt(...]
    all_to_all x1 -> x0, blocking collectives: 10.7 us -> none  [on_device(): lax.all_to_all(patch_result, 'frame', split_axis=0, concat_axis=1, tiled=...]
    dot_general x20 -> x0, matrix products: 8.3 us -> none  [the longest x8 3.1 us: contract_last(): lax.dot_general(left_side, right_side, (((1,), (1,)), ((), ())), preferre...]
    unnamed x19 -> x23, local copies, waits for them, and re-layouts: 3.67 us -> 11.4 us
    all_to_all x1 -> x0, starting transfers between devices: 7.39 us -> none  [on_device(): lax.all_to_all(inner_frames, 'frame', split_axis=1, concat_axis=0, tiled=...]
    all_to_all x1 -> x0, waiting for transfers between devices: 3.76 us -> none  [on_device(): lax.all_to_all(inner_frames, 'frame', split_axis=1, concat_axis=0, tiled=...]
    div x1 -> x0, other arithmetic: 3.09 us -> none  [on_device(): return (result, weight_grads[0] / grad_norm, weight_grads[1] / grad_norm)]
  transfers between devices with their start and end apart: 2 -> 0, of which waited for: 2 -> 0; matrix products, arithmetic and copies ran while one was open for 3% -> 0% of each run, Pallas kernels for 0% -> 0%
where the time goes in v1:
time: 54.8 us; the launch traced here: 54.2 us
  Pallas kernels  39.9 us (73%)
  local copies, waits for them, and re-layouts  11.4 us (21%)
  other arithmetic  2.21 us (4%)
  between operations  0.66 us (1%)
    pallas_call x1, Pallas kernels, on_device(): pl.pallas_call(functools.partial(kernel, n, len(levels), 1.0 / math.sqrt(...  39.9 us
    unnamed x23, local copies, waits for them, and re-layouts  11.4 us
    convert_element_type x1, other arithmetic, on_device(): grad_s[:D].astype(F32)  1.1 us
    convert_element_type x1, other arithmetic, on_device(): grad_t[:D].astype(F32)  1.1 us

profile of v1, /device:TPU:0, one launch (start us, length us, event | category | flops | bytes accessed | tf_op | source)
XLA Modules:
  0.0 54.2 jit_solution(14230465464080319359)
XLA Ops:
  0.6 0.0 copy-start
  0.6 1.4 %copy-done = bf16[512,1536]{1,0:T(8,128)(2,1)S(1)} copy-done((bf16[512,1536]{1,0:T(8,128)(2,1)S(1)}, bf16[512,1536]{1,0:T(8,128)(2,1)}, u32[]{:S(2)}) %copy-start) | copy-done | bytes 1572888
  2.0 0.0 copy-start.1
  2.0 1.4 %copy-done.1 = bf16[512,1536]{1,0:T(8,128)(2,1)S(1)} copy-done((bf16[512,1536]{1,0:T(8,128)(2,1)S(1)}, bf16[512,1536]{1,0:T(8,128)(2,1)}, u32[]{:S(2)}) %copy-start.1) | copy-done | bytes 1572888
  3.5 0.0 copy-start.2
  3.5 1.0 %copy-done.2 = bf16[512,512]{1,0:T(8,128)(2,1)S(1)} copy-done((bf16[512,512]{1,0:T(8,128)(2,1)S(1)}, bf16[512,512]{1,0:T(8,128)(2,1)}, u32[]{:S(2)}) %copy-start.2) | copy-done | bytes 524312
  4.5 0.0 copy-start.3
  4.5 1.0 %copy-done.3 = bf16[512,512]{1,0:T(8,128)(2,1)S(1)} copy-done((bf16[512,512]{1,0:T(8,128)(2,1)S(1)}, bf16[512,512]{1,0:T(8,128)(2,1)}, u32[]{:S(2)}) %copy-start.3) | copy-done | bytes 524312
  5.5 0.0 copy-start.4
  5.5 0.8 %copy-done.4 = bf16[1,64,512]{2,1,0:T(8,128)(2,1)S(1)} copy-done((bf16[1,64,512]{2,1,0:T(8,128)(2,1)S(1)}, bf16[1,64,512]{2,1,0:T(8,128)(2,1)}, u32[]{:S(2)}) %copy-start.4) | copy-done | bytes 65560
  6.4 0.0 copy-start.5
  6.4 0.8 %copy-done.5 = bf16[1,64,512]{2,1,0:T(8,128)(2,1)S(1)} copy-done((bf16[1,64,512]{2,1,0:T(8,128)(2,1)S(1)}, bf16[1,64,512]{2,1,0:T(8,128)(2,1)}, u32[]{:S(2)}) %copy-start.5) | copy-done | bytes 65560
  7.2 0.0 copy-start.6
  7.2 0.8 %copy-done.6 = bf16[1,64,512]{2,1,0:T(8,128)(2,1)S(1)} copy-done((bf16[1,64,512]{2,1,0:T(8,128)(2,1)S(1)}, bf16[1,64,512]{2,1,0:T(8,128)(2,1)}, u32[]{:S(2)}) %copy-start.6) | copy-done | bytes 65560
  8.1 0.0 copy-start.7
  8.1 0.8 %copy-done.7 = bf16[1,64,512]{2,1,0:T(8,128)(2,1)S(1)} copy-done((bf16[1,64,512]{2,1,0:T(8,128)(2,1)S(1)}, bf16[1,64,512]{2,1,0:T(8,128)(2,1)}, u32[]{:S(2)}) %copy-start.7) | copy-done | bytes 65560
  8.9 0.0 copy-start.8
  8.9 0.8 %copy-done.8 = bf16[16,4,512]{2,1,0:T(4,128)(2,1)S(1)} copy-done((bf16[16,4,512]{2,1,0:T(4,128)(2,1)S(1)}, bf16[16,4,512]{2,1,0:T(4,128)(2,1)}, u32[]{:S(2)}) %copy-start.8) | copy-done | bytes 65560
  9.7 0.0 copy-start.9
  9.7 0.8 %copy-done.9 = bf16[16,4,512]{2,1,0:T(4,128)(2,1)S(1)} copy-done((bf16[16,4,512]{2,1,0:T(4,128)(2,1)S(1)}, bf16[16,4,512]{2,1,0:T(4,128)(2,1)}, u32[]{:S(2)}) %copy-start.9) | copy-done | bytes 65560
  10.6 0.0 copy-start.10
  10.6 0.8 %copy-done.10 = bf16[16,4,512]{2,1,0:T(4,128)(2,1)S(1)} copy-done((bf16[16,4,512]{2,1,0:T(4,128)(2,1)S(1)}, bf16[16,4,512]{2,1,0:T(4,128)(2,1)}, u32[]{:S(2)}) %copy-start.10) | copy-done | bytes 65560
  11.4 39.9 %shard_map.130 = (bf16[64,512]{1,0:T(8,128)(2,1)S(1)}, bf16[512,512]{1,0:T(8,128)(2,1)S(1)}, bf16[512,512]{1,0:T(8,128)(2,1)S(1)}) custom-call(bf16[64,512]{1,0:T(8,128)(2,1)S(1)} %bitcast.5, bf16[64,512]{1,0:T(8,128)(2,1)S(1)} %bitcast.6, bf16[64,512]{1,0:T(8,128)(2,1)S(1)} %bitcast.7, bf16[64,512]{1,0:T(8,128)(2,1)S(1)} %bitcast.8, ...), custom_call_target="tpu_custom_call" | custom-call | tf_op jit(solution)/shard_map/pallas_call | solution.py:311
  51.4 1.1 %convert_element_type.6 = f32[512,512]{1,0:T(8,128)} convert(bf16[512,512]{1,0:T(8,128)(2,1)S(1)} %get-tuple-element.7) | non-fusion elementwise | flops 262144 | bytes 1572864 | tf_op jit(solution)/shard_map/convert_element_type | solution.py:333
  52.5 1.1 %convert_element_type.7 = f32[512,512]{1,0:T(8,128)} convert(bf16[512,512]{1,0:T(8,128)(2,1)S(1)} %get-tuple-element.8) | non-fusion elementwise | flops 262144 | bytes 1572864 | tf_op jit(solution)/shard_map/convert_element_type | solution.py:334
  53.6 0.6 %copy.15 = bf16[1,64,512]{2,1,0:T(8,128)(2,1)} copy(bf16[1,64,512]{2,1,0:T(8,128)(2,1)S(1)} %bitcast.9) | data formatting | bytes 131072
Async XLA Ops:
  0.6 1.4 %copy-start = (bf16[512,1536]{1,0:T(8,128)(2,1)S(1)}, bf16[512,1536]{1,0:T(8,128)(2,1)}, u32[]{:S(2)}) copy-start(bf16[512,1536]{1,0:T(8,128)(2,1)} %refs_7_.1) | copy-start | bytes 4718596
  2.0 1.4 %copy-start.1 = (bf16[512,1536]{1,0:T(8,128)(2,1)S(1)}, bf16[512,1536]{1,0:T(8,128)(2,1)}, u32[]{:S(2)}) copy-start(bf16[512,1536]{1,0:T(8,128)(2,1)} %refs_9_.1) | copy-start | bytes 4718596
  3.5 1.0 %copy-start.2 = (bf16[512,512]{1,0:T(8,128)(2,1)S(1)}, bf16[512,512]{1,0:T(8,128)(2,1)}, u32[]{:S(2)}) copy-start(bf16[512,512]{1,0:T(8,128)(2,1)} %refs_8_.1) | copy-start | bytes 1572868
  4.5 1.0 %copy-start.3 = (bf16[512,512]{1,0:T(8,128)(2,1)S(1)}, bf16[512,512]{1,0:T(8,128)(2,1)}, u32[]{:S(2)}) copy-start(bf16[512,512]{1,0:T(8,128)(2,1)} %refs_10_.1) | copy-start | bytes 1572868
  5.5 0.8 %copy-start.4 = (bf16[1,64,512]{2,1,0:T(8,128)(2,1)S(1)}, bf16[1,64,512]{2,1,0:T(8,128)(2,1)}, u32[]{:S(2)}) copy-start(bf16[1,64,512]{2,1,0:T(8,128)(2,1)} %param.11) | copy-start | bytes 196612
  6.4 0.8 %copy-start.5 = (bf16[1,64,512]{2,1,0:T(8,128)(2,1)S(1)}, bf16[1,64,512]{2,1,0:T(8,128)(2,1)}, u32[]{:S(2)}) copy-start(bf16[1,64,512]{2,1,0:T(8,128)(2,1)} %param.12) | copy-start | bytes 196612
  7.2 0.8 %copy-start.6 = (bf16[1,64,512]{2,1,0:T(8,128)(2,1)S(1)}, bf16[1,64,512]{2,1,0:T(8,128)(2,1)}, u32[]{:S(2)}) copy-start(bf16[1,64,512]{2,1,0:T(8,128)(2,1)} %param.13) | copy-start | bytes 196612
  8.1 0.8 %copy-start.7 = (bf16[1,64,512]{2,1,0:T(8,128)(2,1)S(1)}, bf16[1,64,512]{2,1,0:T(8,128)(2,1)}, u32[]{:S(2)}) copy-start(bf16[1,64,512]{2,1,0:T(8,128)(2,1)} %param.14) | copy-start | bytes 196612
  8.9 0.8 %copy-start.8 = (bf16[16,4,512]{2,1,0:T(4,128)(2,1)S(1)}, bf16[16,4,512]{2,1,0:T(4,128)(2,1)}, u32[]{:S(2)}) copy-start(bf16[16,4,512]{2,1,0:T(4,128)(2,1)} %refs_4_.1) | copy-start | bytes 196612
  9.7 0.8 %copy-start.9 = (bf16[16,4,512]{2,1,0:T(4,128)(2,1)S(1)}, bf16[16,4,512]{2,1,0:T(4,128)(2,1)}, u32[]{:S(2)}) copy-start(bf16[16,4,512]{2,1,0:T(4,128)(2,1)} %refs_5_.1) | copy-start | bytes 196612
  10.6 0.8 %copy-start.10 = (bf16[16,4,512]{2,1,0:T(4,128)(2,1)S(1)}, bf16[16,4,512]{2,1,0:T(4,128)(2,1)}, u32[]{:S(2)}) copy-start(bf16[16,4,512]{2,1,0:T(4,128)(2,1)} %refs_6_.1) | copy-start | bytes 196612

commit v2 on v1

--- a/solution.py
+++ b/solution.py
@@ -12,6 +12,7 @@
 HEADS = 8
 HEAD_DIM = D // HEADS
 LANES = 128
+VMEM_LIMIT = 60 * 1024 * 1024
 BF16 = jnp.bfloat16
 F32 = jnp.float32
 
@@ -188,12 +189,12 @@
 
 
 def kernel(n, n_levels, scale, norm, *refs):
-    inputs, refs = refs[:11], refs[11:]
-    result_ref, grad_s_ref, grad_t_ref = refs[:3]
-    refs = refs[3:]
+    inputs, outputs, refs = refs[:11], refs[11:14], refs[14:]
     held, refs = refs[:11], refs[11:]
-    load_sem, out_a, in_a, out_b, in_b, a_send, a_recv, b_send, b_recv = refs[:9]
-    refs = refs[9:]
+    load_sem, store_sem, result, grad_s, grad_t = refs[:5]
+    refs = refs[5:]
+    out_m, in_m, out_a, in_a, out_b, in_b, m_send, m_recv, a_send, a_recv, b_send, b_recv = refs[:12]
+    refs = refs[12:]
     acc_s, send_s = refs[:2]
     recv_s, refs = refs[2 : 2 + n_levels], refs[2 + n_levels :]
     sems_s, refs = refs[:4], refs[4:]
@@ -202,13 +203,6 @@
     sems_t = refs[:4]
 
     me = lax.axis_index("frame")
-    loads = []
-    for i in (1, 2, 3, 0, 8, 4, 5, 6, 7, 10, 9):
-        copy = pltpu.make_async_copy(inputs[i], held[i], load_sem.at[i])
-        copy.start()
-        loads.append((i, copy))
-    loads = dict(loads)
-
     barrier = pltpu.get_barrier_semaphore()
     for d in range(1, n):
         pl.semaphore_signal(
@@ -217,6 +211,10 @@
             device_id={"frame": lax.rem(me + d, n)},
             device_id_type=pl.DeviceIdType.MESH,
         )
+    loads = {}
+    for i in (4, 5, 6, 1, 2, 3, 0, 8, 7, 10, 9):
+        loads[i] = pltpu.make_async_copy(inputs[i], held[i], load_sem.at[i])
+        loads[i].start()
 
     cot_h, qs_h, ks_h, vs_h, qt_h, kt_h, vt_h, wqs_h, wos_h, wqt_h, wot_h = held
     pieces = qt_h.shape[1]
@@ -229,27 +227,10 @@
     def flat(ref):
         return jnp.concatenate([ref[j].astype(F32) for j in range(ref.shape[0])], axis=0).astype(BF16)
 
-    for i in (1, 2, 3, 0):
-        loads[i].wait()
-    cot, q_s, k_s, v_s = cot_h[...], qs_h[...], ks_h[...], vs_h[...]
-    tokens = cot.shape[0]
-    lane = lax.broadcasted_iota(jnp.int32, (tokens, LANES), 1)
-    probs_s, mixed_s = attention_forward(q_s, k_s, v_s, scale, masks, lane, None)
-    partial_s = dot_tn(mixed_s, cot)
-    pl.semaphore_wait(barrier, n - 1)
-    sum_s = GradSum(n, me, acc_s, send_s, grad_s_ref, recv_s, sems_s, norm)
-    sum_s.begin(partial_s)
-
-    loads[8].wait()
-    d_mixed_s = dot_nt(cot, wos_h[...]).astype(BF16)
-    parts_s = attention_backward(q_s, k_s, v_s, d_mixed_s, probs_s, scale, masks, lane)
-    loads[7].wait()
-    d_x1 = (cot.astype(F32) + dot_nt(parts_s, wqs_h[...])).astype(BF16).astype(F32)
-    for j in range(n):
-        out_a[j] = d_x1[j * pieces : (j + 1) * pieces].astype(BF16)
-    sent_a = exchange(n, me, out_a, in_a, a_send, a_recv)
-
-    sum_s.finish_reduce(0)
+    def split(ref, value):
+        for j in range(n):
+            ref[j] = value[j * pieces : (j + 1) * pieces].astype(BF16)
+
     for i in (4, 5, 6):
         loads[i].wait()
     q_t, k_t, v_t = flat(qt_h), flat(kt_h), flat(vt_h)
@@ -260,33 +241,96 @@
     same = lax.rem(key_row, pieces) == lax.rem(query_col, pieces)
     lane_t = lax.broadcasted_iota(jnp.int32, (rows_t, LANES), 1)
     probs_t, mixed_t = attention_forward(q_t, k_t, v_t, scale, masks, lane_t, same)
+    split(out_m, mixed_t.astype(F32))
+
+    for i in (1, 2, 3, 0):
+        loads[i].wait()
+    cot, q_s, k_s, v_s = cot_h[...], qs_h[...], ks_h[...], vs_h[...]
+    tokens = cot.shape[0]
+    lane = lax.broadcasted_iota(jnp.int32, (tokens, LANES), 1)
+    probs_s, mixed_s = attention_forward(q_s, k_s, v_s, scale, masks, lane, None)
+    partial_s = dot_tn(mixed_s, cot)
+    pl.semaphore_wait(barrier, n - 1)
+    sum_s = GradSum(n, me, acc_s, send_s, grad_s, recv_s, sems_s, norm)
+    sum_s.begin(partial_s)
+    sent_m = exchange(n, me, out_m, in_m, m_send, m_recv)
+
+    loads[8].wait()
+    d_mixed_s = dot_nt(cot, wos_h[...]).astype(BF16)
+    parts_s = attention_backward(q_s, k_s, v_s, d_mixed_s, probs_s, scale, masks, lane)
+    sum_s.finish_reduce(0)
+    loads[7].wait()
+    d_x1 = (cot.astype(F32) + dot_nt(parts_s, wqs_h[...])).astype(BF16)
+    split(out_a, d_x1.astype(F32))
+    sent_a = exchange(n, me, out_a, in_a, a_send, a_recv)
+
+    for copy in sent_m:
+        copy.wait()
+    sum_t = GradSum(n, me, acc_t, send_t, grad_t, recv_t, sems_t, norm)
+    sum_t.begin(dot_tn(flat(in_m), d_x1))
+    for level in range(1, n_levels):
+        sum_s.finish_reduce(level)
+    sum_t.finish_reduce(0)
+
     loads[10].wait()
     loads[9].wait()
-    if n_levels > 1:
-        sum_s.finish_reduce(1)
     for copy in sent_a:
         copy.wait()
     rows = flat(in_a)
-
-    sum_t = GradSum(n, me, acc_t, send_t, grad_t_ref, recv_t, sems_t, norm)
-    sum_t.begin(dot_tn(mixed_t, rows))
     d_mixed_t = dot_nt(rows, wot_h[...]).astype(BF16)
     parts_t = attention_backward(q_t, k_t, v_t, d_mixed_t, probs_t, scale, masks, lane_t)
-    d_x0 = rows.astype(F32) + dot_nt(parts_t, wqt_h[...])
-    for j in range(n):
-        out_b[j] = d_x0[j * pieces : (j + 1) * pieces].astype(BF16)
+    if n_levels > 1:
+        sum_t.finish_reduce(1)
+    sum_s.finish_gather(n_levels - 1)
+    split(out_b, rows.astype(F32) + dot_nt(parts_t, wqt_h[...]))
     sent_b = exchange(n, me, out_b, in_b, b_send, b_recv)
 
-    for level in range(n_levels):
+    for level in range(2, n_levels):
         sum_t.finish_reduce(level)
-        if level >= 2:
-            sum_s.finish_reduce(level)
-    for level in reversed(range(n_levels)):
+    for level in reversed(range(n_levels - 1)):
         sum_s.finish_gather(level)
-        sum_t.finish_gather(level)
+    stores = [pltpu.make_async_copy(grad_s, outputs[1], store_sem.at[1])]
+    stores[0].start()
     for copy in sent_b:
         copy.wait()
-    result_ref[...] = flat(in_b)
+    result[...] = flat(in_b)
+    stores.append(pltpu.make_async_copy(result, outputs[0], store_sem.at[0]))
+    stores[1].start()
+    for level in reversed(range(n_levels)):
+        sum_t.finish_gather(level)
+    stores.append(pltpu.make_async_copy(grad_t, outputs[2], store_sem.at[2]))
+    stores[2].start()
+    for store in stores:
+        store.wait()
+
+
+def finish_kernel(result_in, grad_s_in, grad_t_in, result_out, grad_s_out, grad_t_out, half, full, result, sem_in, sem_out):
+    pairs = ((grad_s_in, grad_s_out), (grad_t_in, grad_t_out))
+    parts = 2
+    rows = D // parts
+    loads, stores = [], []
+    for g, (source, _) in enumerate(pairs):
+        for p in range(parts):
+            span = pl.ds(p * rows, rows)
+            copy = pltpu.make_async_copy(source.at[span], half.at[g, span], sem_in.at[g, p])
+            copy.start()
+            loads.append(copy)
+    last = pltpu.make_async_copy(result_in, result, sem_in.at[2, 0])
+    last.start()
+    for g, (_, target) in enumerate(pairs):
+        for p in range(parts):
+            span = pl.ds(p * rows, rows)
+            loads[g * parts + p].wait()
+            full[g, span] = half[g, span].astype(F32)
+            copy = pltpu.make_async_copy(full.at[g, span], target.at[span], sem_out.at[g, p])
+            copy.start()
+            stores.append(copy)
+    last.wait()
+    copy = pltpu.make_async_copy(result, result_out, sem_out.at[2, 0])
+    copy.start()
+    stores.append(copy)
+    for copy in stores:
+        copy.wait()
 
 
 def on_device(n, *args):
@@ -297,9 +341,10 @@
     flat_args = [a.reshape(tokens, width) for a in args[:4]] + list(args[4:])
     levels = reduce_levels(n)
     scratch = [pltpu.VMEM(a.shape, a.dtype) for a in flat_args]
-    scratch.append(pltpu.SemaphoreType.DMA((len(flat_args),)))
-    scratch += [pltpu.VMEM((n, pieces, width), BF16)] * 4
-    scratch += [pltpu.SemaphoreType.DMA((n - 1,))] * 4
+    scratch += [pltpu.SemaphoreType.DMA((len(flat_args),)), pltpu.SemaphoreType.DMA((3,))]
+    scratch += [pltpu.VMEM((tokens, width), BF16)] + [pltpu.VMEM((padded_rows(n), D), BF16)] * 2
+    scratch += [pltpu.VMEM((n, pieces, width), BF16)] * 6
+    scratch += [pltpu.SemaphoreType.DMA((n - 1,))] * 6
     widest = max(size for _, size in levels)
     for _ in range(2):
         scratch += [pltpu.VMEM((padded_rows(n), D), F32), pltpu.VMEM((padded_rows(n), D), BF16)]
@@ -321,18 +366,32 @@
             jax.ShapeDtypeStruct((padded_rows(n), D), BF16),
             jax.ShapeDtypeStruct((padded_rows(n), D), BF16),
         ),
-        in_specs=[pl.BlockSpec(memory_space=pltpu.HBM)] * len(flat_args),
-        out_specs=(pl.BlockSpec(memory_space=pltpu.VMEM),) * 3,
+        in_specs=[pl.BlockSpec(memory_space=pl.ANY)] * len(flat_args),
+        out_specs=(pl.BlockSpec(memory_space=pl.ANY),) * 3,
         scratch_shapes=scratch,
         compiler_params=pltpu.CompilerParams(
-            collective_id=0, has_side_effects=True, vmem_limit_bytes=40 * 1024 * 1024
+            collective_id=0, has_side_effects=True, vmem_limit_bytes=VMEM_LIMIT
         ),
     )(*flat_args)
-    return (
-        result.reshape(frames_here, patches, width),
-        grad_s[:D].astype(F32),
-        grad_t[:D].astype(F32),
-    )
+    result, grad_s, grad_t = pl.pallas_call(
+        finish_kernel,
+        out_shape=(
+            jax.ShapeDtypeStruct((tokens, width), BF16),
+            jax.ShapeDtypeStruct((D, D), F32),
+            jax.ShapeDtypeStruct((D, D), F32),
+        ),
+        in_specs=[pl.BlockSpec(memory_space=pl.ANY)] * 3,
+        out_specs=(pl.BlockSpec(memory_space=pl.ANY),) * 3,
+        scratch_shapes=[
+            pltpu.VMEM((2, D, D), BF16),
+            pltpu.VMEM((2, D, D), F32),
+            pltpu.VMEM((tokens, width), BF16),
+            pltpu.SemaphoreType.DMA((3, 2)),
+            pltpu.SemaphoreType.DMA((3, 2)),
+        ],
+        compiler_params=pltpu.CompilerParams(vmem_limit_bytes=VMEM_LIMIT),
+    )(result, grad_s, grad_t)
+    return result.reshape(frames_here, patches, width), grad_s, grad_t
 
 
 def solution(mesh):

time: 54.8 us -> 43.7 us (0.80)
  local copies, waits for them, and re-layouts: 11.4 us -> 0 us
  Pallas kernels: 39.9 us -> 42.9 us
  other arithmetic: 2.21 us -> 0 us
    unnamed x23 -> x0, local copies, waits for them, and re-layouts: 11.4 us -> none
    pallas_call x0 -> x1, Pallas kernels: none -> 2.41 us  [on_device(): pl.pallas_call(finish_kernel, out_shape=(jax.ShapeDtypeStruct((tokens, wi...]
    convert_element_type x2 -> x0, other arithmetic: 2.21 us -> none  [the longest x1 1.1 us: on_device(): grad_s[:D].astype(F32)]
where the time goes in v2:
time: 43.7 us; the launch traced here: 43.5 us
  Pallas kernels  42.9 us (98%)
  between operations  0.64 us (1%)
    pallas_call x1, Pallas kernels, on_device(): pl.pallas_call(functools.partial(kernel, n, len(levels), 1.0 / math.sqrt(...  40.4 us
    pallas_call x1, Pallas kernels, on_device(): pl.pallas_call(finish_kernel, out_shape=(jax.ShapeDtypeStruct((tokens, wi...  2.41 us

profile of v2, /device:TPU:0, one launch (start us, length us, event | category | flops | bytes accessed | tf_op | source)
XLA Modules:
  0.0 43.5 jit_solution(15673978256332978101)
XLA Ops:
  0.6 40.4 %shard_map.130 = (bf16[64,512]{1,0:T(8,128)(2,1)}, bf16[512,512]{1,0:T(8,128)(2,1)}, bf16[512,512]{1,0:T(8,128)(2,1)}) custom-call(bf16[64,512]{1,0:T(8,128)(2,1)} %bitcast.5, bf16[64,512]{1,0:T(8,128)(2,1)} %bitcast.6, bf16[64,512]{1,0:T(8,128)(2,1)} %bitcast.7, bf16[64,512]{1,0:T(8,128)(2,1)} %bitcast.8, bf16[16,4,512]{2,1,0:T(4,128)(2,1)} %refs_4_.1, ...), custom_call_target="tpu_custom_call" | custom-call | tf_op jit(solution)/shard_map/pallas_call | solution.py:356
  41.1 2.4 %shard_map.131 = (bf16[64,512]{1,0:T(8,128)(2,1)}, f32[512,512]{1,0:T(8,128)}, f32[512,512]{1,0:T(8,128)}) custom-call(bf16[64,512]{1,0:T(8,128)(2,1)} %get-tuple-element.9.result_in, bf16[512,512]{1,0:T(8,128)(2,1)} %get-tuple-element.10.grad_s_in, bf16[512,512]{1,0:T(8,128)(2,1)} %get-tuple-element.11.grad_t_in), custom_call_target="tpu_custom_call" | custom-call | tf_op jit(solution)/shard_map/pallas_call | solution.py:376

commit v3 on v2

--- a/solution.py
+++ b/solution.py
@@ -39,8 +39,12 @@
     return levels
 
 
+PARTS = 2
+PART = D // PARTS
+
+
 def padded_rows(n):
-    return n * 16 * pl.cdiv(D, n * 16)
+    return n * 16 * pl.cdiv(PART, n * 16)
 
 
 def head_stack(tile, group_masks):
@@ -124,11 +128,11 @@
         self.pending = copies
 
     def begin(self, partial):
-        self.acc[:D, :] = partial
-        self.send[:D, :] = partial.astype(BF16)
-        if self.rows[0] > D:
-            self.acc[D:, :] = jnp.zeros((self.rows[0] - D, D), F32)
-            self.send[D:, :] = jnp.zeros((self.rows[0] - D, D), BF16)
+        self.acc[:PART, :] = partial
+        self.send[:PART, :] = partial.astype(BF16)
+        if self.rows[0] > PART:
+            self.acc[PART:, :] = jnp.zeros((self.rows[0] - PART, D), F32)
+            self.send[PART:, :] = jnp.zeros((self.rows[0] - PART, D), BF16)
         self.start_reduce(0)
 
     def finish_reduce(self, level):
@@ -195,14 +199,30 @@
     refs = refs[5:]
     out_m, in_m, out_a, in_a, out_b, in_b, m_send, m_recv, a_send, a_recv, b_send, b_recv = refs[:12]
     refs = refs[12:]
-    acc_s, send_s = refs[:2]
-    recv_s, refs = refs[2 : 2 + n_levels], refs[2 + n_levels :]
-    sems_s, refs = refs[:4], refs[4:]
-    acc_t, send_t = refs[:2]
-    recv_t, refs = refs[2 : 2 + n_levels], refs[2 + n_levels :]
-    sems_t = refs[:4]
-
     me = lax.axis_index("frame")
+    streams = []
+    for i in range(2 * PARTS):
+        acc, send, recv, sems = refs[0], refs[1], refs[2 : 2 + n_levels], refs[2 + n_levels : 6 + n_levels]
+        refs = refs[6 + n_levels :]
+        out = (grad_s if i < PARTS else grad_t).at[i % PARTS]
+        streams.append(GradSum(n, me, acc, send, out, recv, sems, norm))
+    sum_s, sum_t = streams[:PARTS], streams[PARTS:]
+    last = n_levels - 1
+
+    def begin(sums, mixed, rows):
+        for p in range(PARTS):
+            sums[p].begin(dot_tn(mixed[:, p * PART : (p + 1) * PART], rows))
+
+    def reduce(sums, level):
+        if level < n_levels:
+            for part in sums:
+                part.finish_reduce(level)
+
+    def gather(sums, level):
+        if level >= 0:
+            for part in sums:
+                part.finish_gather(level)
+
     barrier = pltpu.get_barrier_semaphore()
     for d in range(1, n):
         pl.semaphore_signal(
@@ -212,7 +232,7 @@
             device_id_type=pl.DeviceIdType.MESH,
         )
     loads = {}
-    for i in (4, 5, 6, 1, 2, 3, 0, 8, 7, 10, 9):
+    for i in (1, 2, 3, 0, 4, 5, 6, 8, 7, 10, 9):
         loads[i] = pltpu.make_async_copy(inputs[i], held[i], load_sem.at[i])
         loads[i].start()
 
@@ -230,6 +250,15 @@
     def split(ref, value):
         for j in range(n):
             ref[j] = value[j * pieces : (j + 1) * pieces].astype(BF16)
+
+    for i in (1, 2, 3, 0):
+        loads[i].wait()
+    cot, q_s, k_s, v_s = cot_h[...], qs_h[...], ks_h[...], vs_h[...]
+    tokens = cot.shape[0]
+    lane = lax.broadcasted_iota(jnp.int32, (tokens, LANES), 1)
+    probs_s, mixed_s = attention_forward(q_s, k_s, v_s, scale, masks, lane, None)
+    pl.semaphore_wait(barrier, n - 1)
+    begin(sum_s, mixed_s, cot)
 
     for i in (4, 5, 6):
         loads[i].wait()
@@ -242,23 +271,13 @@
     lane_t = lax.broadcasted_iota(jnp.int32, (rows_t, LANES), 1)
     probs_t, mixed_t = attention_forward(q_t, k_t, v_t, scale, masks, lane_t, same)
     split(out_m, mixed_t.astype(F32))
-
-    for i in (1, 2, 3, 0):
-        loads[i].wait()
-    cot, q_s, k_s, v_s = cot_h[...], qs_h[...], ks_h[...], vs_h[...]
-    tokens = cot.shape[0]
-    lane = lax.broadcasted_iota(jnp.int32, (tokens, LANES), 1)
-    probs_s, mixed_s = attention_forward(q_s, k_s, v_s, scale, masks, lane, None)
-    partial_s = dot_tn(mixed_s, cot)
-    pl.semaphore_wait(barrier, n - 1)
-    sum_s = GradSum(n, me, acc_s, send_s, grad_s, recv_s, sems_s, norm)
-    sum_s.begin(partial_s)
     sent_m = exchange(n, me, out_m, in_m, m_send, m_recv)
+    reduce(sum_s, 0)
 
     loads[8].wait()
     d_mixed_s = dot_nt(cot, wos_h[...]).astype(BF16)
     parts_s = attention_backward(q_s, k_s, v_s, d_mixed_s, probs_s, scale, masks, lane)
-    sum_s.finish_reduce(0)
+    reduce(sum_s, 1)
     loads[7].wait()
     d_x1 = (cot.astype(F32) + dot_nt(parts_s, wqs_h[...])).astype(BF16)
     split(out_a, d_x1.astype(F32))
@@ -266,11 +285,9 @@
 
     for copy in sent_m:
         copy.wait()
-    sum_t = GradSum(n, me, acc_t, send_t, grad_t, recv_t, sems_t, norm)
-    sum_t.begin(dot_tn(flat(in_m), d_x1))
-    for level in range(1, n_levels):
-        sum_s.finish_reduce(level)
-    sum_t.finish_reduce(0)
+    begin(sum_t, flat(in_m), d_x1)
+    reduce(sum_t, 0)
+    reduce(sum_s, 2)
 
     loads[10].wait()
     loads[9].wait()
@@ -279,16 +296,14 @@
     rows = flat(in_a)
     d_mixed_t = dot_nt(rows, wot_h[...]).astype(BF16)
     parts_t = attention_backward(q_t, k_t, v_t, d_mixed_t, probs_t, scale, masks, lane_t)
-    if n_levels > 1:
-        sum_t.finish_reduce(1)
-    sum_s.finish_gather(n_levels - 1)
+    reduce(sum_t, 1)
+    gather(sum_s, last)
     split(out_b, rows.astype(F32) + dot_nt(parts_t, wqt_h[...]))
     sent_b = exchange(n, me, out_b, in_b, b_send, b_recv)
 
-    for level in range(2, n_levels):
-        sum_t.finish_reduce(level)
-    for level in reversed(range(n_levels - 1)):
-        sum_s.finish_gather(level)
+    reduce(sum_t, 2)
+    for level in reversed(range(last)):
+        gather(sum_s, level)
     stores = [pltpu.make_async_copy(grad_s, outputs[1], store_sem.at[1])]
     stores[0].start()
     for copy in sent_b:
@@ -297,7 +312,7 @@
     stores.append(pltpu.make_async_copy(result, outputs[0], store_sem.at[0]))
     stores[1].start()
     for level in reversed(range(n_levels)):
-        sum_t.finish_gather(level)
+        gather(sum_t, level)
     stores.append(pltpu.make_async_copy(grad_t, outputs[2], store_sem.at[2]))
     stores[2].start()
     for store in stores:
@@ -306,13 +321,12 @@
 
 def finish_kernel(result_in, grad_s_in, grad_t_in, result_out, grad_s_out, grad_t_out, half, full, result, sem_in, sem_out):
     pairs = ((grad_s_in, grad_s_out), (grad_t_in, grad_t_out))
-    parts = 2
-    rows = D // parts
+    parts, rows = PARTS, PART
     loads, stores = [], []
     for g, (source, _) in enumerate(pairs):
         for p in range(parts):
             span = pl.ds(p * rows, rows)
-            copy = pltpu.make_async_copy(source.at[span], half.at[g, span], sem_in.at[g, p])
+            copy = pltpu.make_async_copy(source.at[p, pl.ds(0, rows)], half.at[g, span], sem_in.at[g, p])
             copy.start()
             loads.append(copy)
     last = pltpu.make_async_copy(result_in, result, sem_in.at[2, 0])
@@ -342,11 +356,11 @@
     levels = reduce_levels(n)
     scratch = [pltpu.VMEM(a.shape, a.dtype) for a in flat_args]
     scratch += [pltpu.SemaphoreType.DMA((len(flat_args),)), pltpu.SemaphoreType.DMA((3,))]
-    scratch += [pltpu.VMEM((tokens, width), BF16)] + [pltpu.VMEM((padded_rows(n), D), BF16)] * 2
+    scratch += [pltpu.VMEM((tokens, width), BF16)] + [pltpu.VMEM((PARTS, padded_rows(n), D), BF16)] * 2
     scratch += [pltpu.VMEM((n, pieces, width), BF16)] * 6
     scratch += [pltpu.SemaphoreType.DMA((n - 1,))] * 6
     widest = max(size for _, size in levels)
-    for _ in range(2):
+    for _ in range(2 * PARTS):
         scratch += [pltpu.VMEM((padded_rows(n), D), F32), pltpu.VMEM((padded_rows(n), D), BF16)]
         rows = padded_rows(n)
         for _, size in levels:
@@ -363,8 +377,8 @@
         ),
         out_shape=(
             jax.ShapeDtypeStruct((tokens, width), BF16),
-            jax.ShapeDtypeStruct((padded_rows(n), D), BF16),
-            jax.ShapeDtypeStruct((padded_rows(n), D), BF16),
+            jax.ShapeDtypeStruct((PARTS, padded_rows(n), D), BF16),
+            jax.ShapeDtypeStruct((PARTS, padded_rows(n), D), BF16),
         ),
         in_specs=[pl.BlockSpec(memory_space=pl.ANY)] * len(flat_args),
         out_specs=(pl.BlockSpec(memory_space=pl.ANY),) * 3,

time: 43.7 us -> 39.7 us (0.908)
  Pallas kernels: 42.9 us -> 38.9 us
    pallas_call x1, Pallas kernels: 40.4 us -> 36.4 us  [on_device(): pl.pallas_call(functools.partial(kernel, n, len(levels), 1.0 / math.sqrt(...]
where the time goes in v3:
time: 39.7 us; the launch traced here: 39.5 us
  Pallas kernels  38.9 us (98%)
  between operations  0.64 us (2%)
    pallas_call x1, Pallas kernels, on_device(): pl.pallas_call(functools.partial(kernel, n, len(levels), 1.0 / math.sqrt(...  36.4 us
    pallas_call x1, Pallas kernels, on_device(): pl.pallas_call(finish_kernel, out_shape=(jax.ShapeDtypeStruct((tokens, wi...  2.41 us

profile of v3, /device:TPU:0, one launch (start us, length us, event | category | flops | bytes accessed | tf_op | source)
XLA Modules:
  0.0 39.5 jit_solution(13248282635508859974)
XLA Ops:
  0.6 36.4 %shard_map.130 = (bf16[64,512]{1,0:T(8,128)(2,1)}, bf16[2,256,512]{2,1,0:T(8,128)(2,1)}, bf16[2,256,512]{2,1,0:T(8,128)(2,1)}) custom-call(bf16[64,512]{1,0:T(8,128)(2,1)} %bitcast.5, bf16[64,512]{1,0:T(8,128)(2,1)} %bitcast.6, bf16[64,512]{1,0:T(8,128)(2,1)} %bitcast.7, bf16[64,512]{1,0:T(8,128)(2,1)} %bitcast.8, bf16[16,4,512]{2,1,0:T(4,128)(2,1)} %refs_4_.1, ...), custom_call_target="tpu_custom_call" | custom-call | tf_op jit(solution)/shard_map/pallas_call | solution.py:370
  37.1 2.4 %shard_map.131 = (bf16[64,512]{1,0:T(8,128)(2,1)}, f32[512,512]{1,0:T(8,128)}, f32[512,512]{1,0:T(8,128)}) custom-call(bf16[64,512]{1,0:T(8,128)(2,1)} %get-tuple-element.9.result_in, bf16[2,256,512]{2,1,0:T(8,128)(2,1)} %get-tuple-element.10.grad_s_in, bf16[2,256,512]{2,1,0:T(8,128)(2,1)} %get-tuple-element.11.grad_t_in), custom_call_target="tpu_custom_call" | custom-call | tf_op jit(solution)/shard_map/pallas_call | solution.py:390

commit v4 on v3

--- a/solution.py
+++ b/solution.py
@@ -277,11 +277,11 @@
     loads[8].wait()
     d_mixed_s = dot_nt(cot, wos_h[...]).astype(BF16)
     parts_s = attention_backward(q_s, k_s, v_s, d_mixed_s, probs_s, scale, masks, lane)
-    reduce(sum_s, 1)
     loads[7].wait()
     d_x1 = (cot.astype(F32) + dot_nt(parts_s, wqs_h[...])).astype(BF16)
     split(out_a, d_x1.astype(F32))
     sent_a = exchange(n, me, out_a, in_a, a_send, a_recv)
+    reduce(sum_s, 1)
 
     for copy in sent_m:
         copy.wait()
@@ -294,15 +294,17 @@
     for copy in sent_a:
         copy.wait()
     rows = flat(in_a)
+    reduce(sum_t, 1)
+    gather(sum_s, last)
     d_mixed_t = dot_nt(rows, wot_h[...]).astype(BF16)
     parts_t = attention_backward(q_t, k_t, v_t, d_mixed_t, probs_t, scale, masks, lane_t)
-    reduce(sum_t, 1)
-    gather(sum_s, last)
     split(out_b, rows.astype(F32) + dot_nt(parts_t, wqt_h[...]))
     sent_b = exchange(n, me, out_b, in_b, b_send, b_recv)
 
     reduce(sum_t, 2)
-    for level in reversed(range(last)):
+    gather(sum_s, last - 1)
+    gather(sum_t, last)
+    for level in reversed(range(last - 1)):
         gather(sum_s, level)
     stores = [pltpu.make_async_copy(grad_s, outputs[1], store_sem.at[1])]
     stores[0].start()
@@ -311,7 +313,7 @@
     result[...] = flat(in_b)
     stores.append(pltpu.make_async_copy(result, outputs[0], store_sem.at[0]))
     stores[1].start()
-    for level in reversed(range(n_levels)):
+    for level in reversed(range(last)):
         gather(sum_t, level)
     stores.append(pltpu.make_async_copy(grad_t, outputs[2], store_sem.at[2]))
     stores[2].start()

time: 39.7 us -> 38.7 us (0.975)
  Pallas kernels: 38.9 us -> 37.9 us
    pallas_call x1, Pallas kernels: 36.4 us -> 35.5 us  [on_device(): pl.pallas_call(functools.partial(kernel, n, len(levels), 1.0 / math.sqrt(...]
where the time goes in v4:
time: 38.7 us; the launch traced here: 38.6 us
  Pallas kernels  37.9 us (98%)
  between operations  0.64 us (2%)
    pallas_call x1, Pallas kernels, on_device(): pl.pallas_call(functools.partial(kernel, n, len(levels), 1.0 / math.sqrt(...  35.5 us
    pallas_call x1, Pallas kernels, on_device(): pl.pallas_call(finish_kernel, out_shape=(jax.ShapeDtypeStruct((tokens, wi...  2.41 us

profile of v4, /device:TPU:0, one launch (start us, length us, event | category | flops | bytes accessed | tf_op | source)
XLA Modules:
  0.0 38.6 jit_solution(6023909644957276890)
XLA Ops:
  0.6 35.5 %shard_map.130 = (bf16[64,512]{1,0:T(8,128)(2,1)}, bf16[2,256,512]{2,1,0:T(8,128)(2,1)}, bf16[2,256,512]{2,1,0:T(8,128)(2,1)}) custom-call(bf16[64,512]{1,0:T(8,128)(2,1)} %bitcast.5, bf16[64,512]{1,0:T(8,128)(2,1)} %bitcast.6, bf16[64,512]{1,0:T(8,128)(2,1)} %bitcast.7, bf16[64,512]{1,0:T(8,128)(2,1)} %bitcast.8, bf16[16,4,512]{2,1,0:T(4,128)(2,1)} %refs_4_.1, ...), custom_call_target="tpu_custom_call" | custom-call | tf_op jit(solution)/shard_map/pallas_call | solution.py:372
  36.1 2.4 %shard_map.131 = (bf16[64,512]{1,0:T(8,128)(2,1)}, f32[512,512]{1,0:T(8,128)}, f32[512,512]{1,0:T(8,128)}) custom-call(bf16[64,512]{1,0:T(8,128)(2,1)} %get-tuple-element.9.result_in, bf16[2,256,512]{2,1,0:T(8,128)(2,1)} %get-tuple-element.10.grad_s_in, bf16[2,256,512]{2,1,0:T(8,128)(2,1)} %get-tuple-element.11.grad_t_in), custom_call_target="tpu_custom_call" | custom-call | tf_op jit(solution)/shard_map/pallas_call | solution.py:392
